TPU v7x, 256 devices: a whole 4x4x8 slice. The times are simulated.
256 devices in a mesh: dp: 128 (over y, x, z), proto: 2 (over core).
Axes of the slice: x: 4, y: 4, z: 8, core: 2. Of those that a mesh axis runs over, the one named last changes fastest.
Arguments:
- teacher_feats: bfloat16 [1536, 2, 256], P('dp'), may hold values from -3 to 3
- student_feats: bfloat16 [1536, 10, 256], P('dp'), may hold values from -1 to 1
- proto_v: bfloat16 [256, 65536], P(None, ('dp', 'proto')), may hold values from -1 to 1
Outputs:
- row_loss: float32 [1536, 10], P('dp')
- grad_student: float32 [1536, 10, 256], P('dp')
- grad_v: float32 [256, 65536], P(None, ('dp', 'proto'))
All inputs are finite; a program needn't handle non-finite values.
Results may differ from a plain program's by a relative error of at most 0.0022.
Values may be sent and summed in bfloat16 or wider, within the bound.
A program may use at most 192 MiB of HBM per device.

v0:
```python
import jax
import jax.numpy as jnp
from jax import lax
from jax.sharding import PartitionSpec as P

SWEEPS = 3


epsilon = 1e-12
teacher_temp = 0.07
student_temp = 0.1


def targets_mix(targets, crop_count):
    first_crop = targets[:, 0]
    second_crop = targets[:, 1]
    average = (first_crop + second_crop) * 0.5
    locals_part = jnp.broadcast_to(
        average[:, None, :], (average.shape[0], crop_count - 2, average.shape[1])
    )
    return jnp.concatenate([second_crop[:, None, :], first_crop[:, None, :], locals_part], axis=1)


def project_rows(grad_rows, student_f, snorm):
    return (grad_rows - student_f * jnp.sum(student_f * grad_rows, axis=-1, keepdims=True)) / snorm


def shards(teacher_feats, student_feats, proto_v):
    own_images, teacher_count, feat_width = teacher_feats.shape
    crop_count = student_feats.shape[1]
    own_cols = proto_v.shape[1]
    proto_f = proto_v.astype(jnp.float32)
    colnorm = jnp.sqrt(jnp.sum(proto_f * proto_f, axis=0, keepdims=True) + epsilon)
    weight_f = proto_f / colnorm
    weight_b = weight_f.astype(jnp.bfloat16)
    teacher_f = teacher_feats.reshape(own_images * teacher_count, feat_width).astype(jnp.float32)
    teacher_n = (
        teacher_f / jnp.sqrt(jnp.sum(teacher_f * teacher_f, axis=1, keepdims=True) + epsilon)
    ).astype(jnp.bfloat16)
    student_raw = student_feats.astype(jnp.float32)
    snorm = jnp.sqrt(jnp.sum(student_raw * student_raw, axis=-1, keepdims=True) + epsilon)
    student_f = student_raw / snorm
    student_b = student_f.astype(jnp.bfloat16).reshape(own_images * crop_count, feat_width)
    every_teacher, every_student = (
        lax.all_gather(teacher_n, "dp", axis=0, tiled=True),
        lax.all_gather(student_b, "dp", axis=0, tiled=True),
    )
    all_images = every_teacher.shape[0] // teacher_count
    teacher_scores = jnp.dot(every_teacher, weight_b, preferred_element_type=jnp.float32)
    student_scores = jnp.dot(every_student, weight_b, preferred_element_type=jnp.float32)
    targets = jnp.exp(teacher_scores / teacher_temp)
    for sweep_index in range(SWEEPS):
        targets = targets / jnp.sum(targets, axis=0, keepdims=True)
        row_total = lax.psum(jnp.sum(targets, axis=1), ("dp", "proto"))
        targets = targets / row_total[:, None]
    targets = targets.reshape(all_images, teacher_count, own_cols)
    logits = student_scores.reshape(all_images, crop_count, own_cols) / student_temp
    exponent = jnp.exp(logits)
    zsum = lax.psum(jnp.sum(exponent, axis=-1), ("dp", "proto"))[:, :, None]
    prob = exponent / zsum
    logp = logits - jnp.log(zsum)
    mixed = targets_mix(targets, crop_count)
    loss_flat = (-jnp.sum(mixed * logp, axis=-1)).reshape(all_images * crop_count)
    dlogit = (
        ((prob - mixed) / student_temp)
        .astype(jnp.bfloat16)
        .reshape(all_images * crop_count, own_cols)
    )
    grad_w = lax.dot_general(
        every_student, dlogit, (((0,), (0,)), ((), ())), preferred_element_type=jnp.float32
    )
    grad_v = (grad_w - weight_f * jnp.sum(weight_f * grad_w, axis=0, keepdims=True)) / colnorm
    grad_part = lax.dot_general(
        dlogit, weight_b, (((1,), (1,)), ((), ())), preferred_element_type=jnp.float32
    )
    summed, loss_sum = (
        lax.psum_scatter(grad_part, "dp", scatter_dimension=0, tiled=True),
        lax.psum_scatter(loss_flat, "dp", scatter_dimension=0, tiled=True),
    )
    grad_n, row_loss = lax.psum((summed, loss_sum), "proto")
    grad_n = grad_n.reshape(own_images, crop_count, feat_width)
    grad_student = project_rows(grad_n, student_f, snorm)
    row_loss = row_loss.reshape(own_images, crop_count)
    return (row_loss, grad_student, grad_v)


def solution(mesh):
    in_specs = (P("dp", None, None), P("dp", None, None), P(None, ("dp", "proto")))
    out_specs = (P("dp", None), P("dp", None, None), P(None, ("dp", "proto")))
    return jax.shard_map(shards, mesh=mesh, in_specs=in_specs, out_specs=out_specs, check_vma=False)
```

profile of v0, /device:TPU:1, one launch (start us, length us, event | category | flops | bytes accessed | tf_op | source)
XLA Modules:
  0.0 1499.0 jit_solution(17712158670607209364)
XLA Ops:
  7.2 0.8 multiply_reduce_fusion.3
  8.0 0.7 reshape.74
  8.7 0.1 sqrt.28
  8.8 0.7 divide_convert_fusion
  9.6 1.0 fusion.17
  10.6 1.0 fusion.20
  11.6 0.7 reshape.71
  12.3 1.0 fusion.16
  13.3 102.3 %all-gather.3.cloned.1.call-done = bf16[3072,256]{1,0:T(8,128)(2,1)} async-done(((bf16[24,256]{1,0:T(8,128)(2,1)}), bf16[3072,256]{1,0:T(8,128)(2,1)}) %all-gather.3.cloned.1.call-update) | async-done | bytes 1572880 | tf_op jit(solution)/shard_map/all_gather | solution.py:45
  115.6 2.2 fusion.26
  117.8 0.5 divide_reduce_fusion
  118.3 79.8 %psum.42 = f32[3072]{0:T(1024)S(1)} all-reduce(f32[3072]{0:T(1024)S(1)} %divide_reduce_fusion), channel_id=1, replica_groups=mesh['dp'=128,'proto'=2] {'dp','proto'}, use_global_device_ids=true, to_apply=%region_4.0 | all-reduce | flops 3072 | bytes 24576 | tf_op jit(solution)/shard_map/psum | solution.py:54
  198.1 0.5 fusion.9
  198.6 1.9 fusion.10
  200.5 73.6 %psum.43 = f32[3072]{0:T(1024)S(1)} all-reduce(f32[3072]{0:T(1024)S(1)} %fusion.10), channel_id=1, replica_groups=mesh['dp'=128,'proto'=2] {'dp','proto'}, use_global_device_ids=true, to_apply=%region_7.0 | all-reduce | flops 3072 | bytes 24576 | tf_op jit(solution)/shard_map/psum | solution.py:54
  274.1 1.6 fusion.11
  275.8 2.9 fusion.12
  278.6 11.8 exponential_reduce_fusion
  290.4 1.7 reduce_sum.129
  292.1 0.2 reduce-scatter.2.cloned.1.call-start
  292.4 248.7 %all-reduce.7.cloned.1.call-done = (f32[3072]{0:T(1024)}, f32[1536,10]{1,0:T(8,128)}) async-done(((f32[3072]{0:T(1024)}, f32[1536,10]{1,0:T(8,128)}), (f32[3072]{0:T(1024)}, f32[1536,10]{1,0:T(8,128)})) %all-reduce.7.cloned.1.call-update) | async-done | bytes 73744 | tf_op jit(solution)/shard_map/psum | solution.py:54
  541.1 1.7 div.128
  542.8 2.1 log.4
  544.9 4.7 fusion.8
  549.6 3.7 reshape.70
  553.3 1.7 sub.21
  555.0 3.3 fusion.25
  558.3 0.1 copy.32
  558.5 0.9 broadcast_in_dim.5
  559.4 10.0 pad_maximum_fusion
  569.4 21.3 %concatenate.6 = f32[15360,256]{1,0:T(8,128)} reshape(f32[1536,10,256]{2,1,0:T(8,128)} %pad_maximum_fusion) | data formatting | bytes 31457280 | tf_op jit(solution)/shard_map/concatenate | solution.py:21
  590.7 15.6 %copy.15 = f32[15360,256]{0,1:T(8,128)} copy(f32[15360,256]{1,0:T(8,128)} %concatenate.6) | data formatting | bytes 31457280 | tf_op jit(solution)/shard_map/concatenate | solution.py:21
  606.4 11.5 multiply_convert_fusion
  617.9 3.1 copy-done
  621.0 7.8 fusion.21
  628.8 0.6 copy-done.3
  629.4 0.6 dynamic-slice
  630.7 578.1 %all-reduce = f32[15360]{0:T(1024)S(1)} all-reduce(f32[15360]{0:T(1024)S(1)} %neg.4), channel_id=2, replica_groups=mesh['dp'=128,'proto'=2] {'dp'}, use_global_device_ids=true, to_apply=%region_15.0.clone | all-reduce | flops 15360 | bytes 122880
  1208.7 0.1 dynamic-slice.1
  1208.8 0.1 reshape.72
  1208.9 110.2 %psum.46 = f32[12,10]{1,0:T(8,128)} all-reduce(f32[12,10]{1,0:T(8,128)S(1)} %reshape.72), channel_id=1, replica_groups=mesh['dp'=128,'proto'=2] {'proto'}, use_global_device_ids=true, to_apply=%region_16.0 | all-reduce | flops 120 | bytes 960 | tf_op jit(solution)/shard_map/psum | solution.py:80
  1319.1 7.8 multiply_reduce_fusion.1
  1326.9 128.3 %reduce-scatter.2.cloned.1.call-done = f32[120,256]{1,0:T(8,128)} async-done(((f32[15360,256]{1,0:T(8,128)}), f32[120,256]{1,0:T(8,128)}) %reduce-scatter.2.cloned.1.call-update) | async-done | bytes 122896 | tf_op jit(solution)/shard_map/reduce_scatter | solution.py:77
  1455.3 1.6 reshape.73
  1456.9 0.8 subtract_divide_fusion
  1457.6 32.2 %all-reduce.5.cloned.1.call-done = f32[12,10,256]{2,1,0:T(8,128)} async-done(((f32[12,10,256]{2,1,0:T(8,128)}), f32[12,10,256]{2,1,0:T(8,128)}) %all-reduce.5.cloned.1.call-update) | async-done | bytes 122896 | tf_op jit(solution)/shard_map/psum | solution.py:80
  1489.8 1.9 fusion.15
  1491.8 0.7 copy.17
  (20 shorter events, 0.3 us)
Async XLA Ops:
  7.2 108.4 %all-gather.3.cloned.1.call-start = ((), (), s32[]{:S(2)}) async-start(), calls=%async_computation.1 | async-start | bytes 1585152 | tf_op jit(solution)/shard_map/all_gather | solution.py:45
  9.5 269.1 %all-gather.5.cloned.1.call-start = ((), (), s32[]{:S(2)}) async-start(), calls=%async_computation.2 | async-start | bytes 7925760 | tf_op jit(solution)/shard_map/all_gather | solution.py:46
  12.3 528.8 %all-reduce.7.cloned.1.call-start = ((), (), s32[]{:S(2)}) async-start(), calls=%async_computation.5 | async-start | bytes 1597440 | tf_op jit(solution)/shard_map/psum | solution.py:54
  274.1 4.5 copy-start.1
  292.1 1163.1 %reduce-scatter.2.cloned.1.call-start = ((), (), s32[]{:S(2)}) async-start(), calls=%async_computation.3 | async-start | bytes 15851520 | tf_op jit(solution)/shard_map/reduce_scatter | solution.py:77
  617.9 3.1 copy-start
  628.7 0.7 copy-start.3
  628.8 861.1 %all-reduce.5.cloned.1.call-start = ((), (), s32[]{:S(2)}) async-start(), calls=%async_computation.4 | async-start | bytes 393216 | tf_op jit(solution)/shard_map/psum | solution.py:80
  1319.1 170.7 %copy-start.2 = (bf16[12,10,256]{2,0,1:T(8,128)(2,1)S(1)}, bf16[12,10,256]{2,0,1:T(8,128)(2,1)}, u32[]{:S(2)}) copy-start(bf16[12,10,256]{2,0,1:T(8,128)(2,1)} %param.4) | copy-start | bytes 184324
Sparse Core Ops, SparseCore 0:
  12.0 103.5 all-gather.2
  119.8 124.2 all-gather.4
  292.3 248.7 all-reduce.6
  628.9 826.3 reduce-scatter.1
  1457.7 32.0 all-reduce.4
where the time goes:
time: 1500 us
  blocking collectives  842 us (56%)
  waiting for transfers between devices  512 us (34%)
  local copies, waits for them, and re-layouts  57.1 us (4%)
  other arithmetic  44.1 us (3%)
  matrix products  29.5 us (2%)
    unnamed x1, blocking collectives  578 us
    psum x1, waiting for transfers between devices, shards(): row_total = lax.psum(jnp.sum(targets, axis=1), ('dp', 'proto'))  249 us
    psum x2, blocking collectives, shards(): row_total = lax.psum(jnp.sum(targets, axis=1), ('dp', 'proto'))  153 us
    reduce_scatter x1, waiting for transfers between devices, shards(): lax.psum_scatter(grad_part, 'dp', scatter_dimension=0, tiled=True)  128 us
    psum x1, blocking collectives, shards(): grad_n, row_loss = lax.psum((summed, loss_sum), 'proto')  110 us
    all_gather x1, waiting for transfers between devices, shards(): lax.all_gather(teacher_n, 'dp', axis=0, tiled=True)  102 us
    concatenate x2, local copies, waits for them, and re-layouts, targets_mix(): jnp.concatenate([second_crop[:, None, :], first_crop[:, None, :], locals_...  37 us
    psum x1, waiting for transfers between devices, shards(): grad_n, row_loss = lax.psum((summed, loss_sum), 'proto')  32.2 us
  transfers between devices with their start and end apart: 5, of which 4 were waited for; matrix products, arithmetic and copies ran while one was open for 1% of the time, Pallas kernels for 0%

commit v1 on v0

v1 whole, which is shorter than its diff:
```python
import math

import jax
import jax.numpy as jnp
import numpy as np
from jax import lax
from jax.experimental import pallas as pl
from jax.experimental.pallas import tpu as pltpu
from jax.sharding import PartitionSpec as P

MESH = pl.DeviceIdType.MESH
F32, BF16 = jnp.float32, jnp.bfloat16

epsilon = 1e-12
teacher_temp = 0.07
student_temp = 0.1
LOG2E = math.log2(math.e)

NY, NB, NA = 4, 32, 8
D = 256
PB = 256
SB, TB = 64, 16
SROWS, TROWS = SB * NB, TB * NB
IMG, CROPS, TEACH = 6, 10, 2
SWEEPS = 3
ST = 512
OUTW = D + 128


def mixing():
    m = np.zeros((SB, TB), np.float32)
    for img in range(IMG):
        for crop in range(CROPS):
            row, first = img * CROPS + crop, img * TEACH
            if crop == 0:
                m[row, first + 1] = 1.0
            elif crop == 1:
                m[row, first] = 1.0
            else:
                m[row, first] = m[row, first + 1] = 0.5
    return m


def dot(x, y, dims=((1,), (0,)), precision=None):
    return lax.dot_general(x, y, (dims, ((), ())), preferred_element_type=F32, precision=precision)


def wait_bytes(ref, sem):
    pltpu.make_async_copy(ref, ref, sem).wait()


def column(row):
    return jnp.broadcast_to(row, (128, 128)).T


def kernel(t_ref, s_ref, p_ref, mix_big_ref, mix_ref, out_ref, gv_ref,
           wg, tg, sg, k3, kv, e3, st_ref, szt, ub, gb, gr, hb, hr, gw, cs, cr, ys, yr,
           colbuf, rowbuf, zbuf, ztmp,
           w_ss, w_rs, t_ss, t_rs, s_ss, s_rs, col_ss, col_rs, row_ss, row_rs, z_ss, z_rs,
           g_ss, g_rs, h_ss, h_rs, c_ss, c_rs, y_ss, y_rs, o_ss, o_rs):
    dp = lax.axis_index("dp")
    c = lax.axis_index("proto")
    y, b = dp // NB, dp % NB
    a = y * 2 + c

    def a_dev(a2):
        return ((a2 // 2) * NB + b, a2 % 2)

    def b_dev(b2):
        return (y * NB + b2, c)

    def a_peer(o):
        return (a + o) % NA

    def b_peer(o):
        return (b + o) % NB

    def rows(i, n):
        return pl.ds(pl.multiple_of(i * n, n), n)

    def remote(src, dst, ss, rs, device):
        return pltpu.make_async_remote_copy(
            src_ref=src, dst_ref=dst, send_sem=ss, recv_sem=rs, device_id=device, device_id_type=MESH
        )

    barrier = pltpu.get_barrier_semaphore()

    @pl.loop(1, NA)
    def _(o):
        pl.semaphore_signal(barrier, inc=1, device_id=a_dev(a_peer(o)), device_id_type=MESH)

    @pl.loop(1, NB)
    def _(o):
        pl.semaphore_signal(barrier, inc=1, device_id=b_dev(b_peer(o)), device_id_type=MESH)

    proto_f = p_ref[...].astype(F32)
    colnorm = jnp.sqrt(jnp.sum(proto_f * proto_f, axis=0, keepdims=True) + epsilon)
    wg[a] = (proto_f / colnorm).astype(BF16)
    t_f = t_ref[...].astype(F32)
    tg[rows(b, TB), :] = (
        t_f / jnp.sqrt(jnp.sum(t_f * t_f, axis=1, keepdims=True) + epsilon)
    ).astype(BF16)
    s_raw = s_ref[...].astype(F32)
    snorm = jnp.sqrt(jnp.sum(s_raw * s_raw, axis=1, keepdims=True) + epsilon)
    sg[rows(b, SB), :] = (s_raw / snorm).astype(BF16)

    pl.semaphore_wait(barrier, NA - 1 + NB - 1)

    w_copies = []
    for o in range(1, NY):
        cp = remote(wg.at[a], wg.at[a], w_ss.at[o - 1], w_rs.at[a], a_dev(a_peer(2 * o)))
        cp.start()
        w_copies.append(cp)

    def b_all(src, dst, ss, rs):
        @pl.loop(1, NB)
        def _(o):
            remote(src(b_peer(o)), dst, ss, rs, b_dev(b_peer(o))).start()

    t_own = tg.at[rows(b, TB), :]
    b_all(lambda _: t_own, t_own, t_ss, t_rs)
    cp = remote(wg.at[a], wg.at[a], w_ss.at[NY - 1], w_rs.at[a], (dp, 1 - c))
    cp.start()
    w_copies.append(cp)
    s_own = sg.at[rows(b, SB), :]
    b_all(lambda _: s_own, s_own, s_ss, s_rs)

    for o in range(1, NY):
        a2 = a_peer(2 * (NY - o))
        wait_bytes(wg.at[a2], w_rs.at[a2])
        cp = remote(wg.at[a2], wg.at[a2], w_ss.at[NY - 1 + o], w_rs.at[a2], (dp, 1 - c))
        cp.start()
        w_copies.append(cp)
    for y2 in range(NY):
        a2 = y2 * 2 + 1 - c
        wait_bytes(wg.at[a2], w_rs.at[a2])
    wait_bytes(tg.at[pl.ds(0, (NB - 1) * TB), :], t_rs)

    valid = (lax.broadcasted_iota(jnp.int32, (1, TROWS), 1) % TB < IMG * TEACH).astype(F32)

    def set_u(u_row):
        for r in range(TROWS // 128):
            ub[r * 128:(r + 1) * 128, :] = column(u_row[:, r * 128:(r + 1) * 128])

    set_u(valid)

    def col_send(sweep):
        src = colbuf.at[sweep, a]

        @pl.loop(1, NA)
        def _(o):
            remote(src, src, col_ss.at[sweep], col_rs.at[sweep], a_dev(a_peer(o))).start()

    def col_wait(sweep):
        wait_bytes(colbuf.at[sweep, pl.ds(0, NA - 1)], col_rs.at[sweep])
        total = colbuf[sweep, 0]
        for i in range(1, NA):
            total = total + colbuf[sweep, i]
        return 1.0 / total

    def row_send(sweep):
        src = rowbuf.at[sweep, b]
        b_all(lambda _: src, src, row_ss.at[sweep], row_rs.at[sweep])

    def row_wait(sweep):
        wait_bytes(rowbuf.at[sweep, pl.ds(0, NB - 1)], row_rs.at[sweep])
        total = rowbuf[sweep, 0]
        for i in range(1, NB):
            total = total + rowbuf[sweep, i]
        return valid / total

    def col_part(sweep):
        @pl.loop(0, NA)
        def _(i):
            u2 = ub[...]
            part = jnp.sum(k3[i] * jnp.concatenate([u2, u2], axis=1), axis=0, keepdims=True)
            colbuf[sweep, a, :, rows(i, PB)] = part

    def row_part(sweep, v, last):
        @pl.loop(0, TROWS // 128)
        def _(r):
            acc = jnp.zeros((128, 128), F32)
            h = jnp.zeros((128, D), F32)
            for i in range(NA):
                scaled = k3[i, rows(r, 128), :] * v[:, i * PB:(i + 1) * PB]
                acc = acc + scaled[:, :128] + scaled[:, 128:]
                if last:
                    scaled = scaled.astype(BF16)
                    kv[i, rows(r, 128), :] = scaled
                    h = h + dot(scaled, wg[i], ((1,), (1,)))
            rowbuf[sweep, b, :, rows(r, 128)] = jnp.sum(acc.T, axis=0, keepdims=True)
            if last:
                hb[rows(r, 128), :] = h.astype(BF16)

    @pl.loop(0, NA)
    def _(i):
        k3[i] = jnp.exp2(dot(tg[...], wg[i]) * (LOG2E / teacher_temp))

    def student(step):
        @pl.loop(step, step + 1)
        def _(r):
            x = sg[rows(r, ST), :]
            z = jnp.zeros((ST, 128), F32)
            g = jnp.zeros((ST, D), F32)
            for i in range(NA):
                e = jnp.exp2(dot(x, wg[i]) * (LOG2E / student_temp))
                z = z + e[:, :128] + e[:, 128:]
                e = e.astype(BF16)
                e3[i, rows(r, ST), :] = e
                g = g + dot(e, wg[i], ((1,), (1,)))
            gb[rows(r, ST), :] = g.astype(BF16)
            for j in range(ST // 128):
                part = jnp.sum(z[j * 128:(j + 1) * 128, :].T, axis=0, keepdims=True)
                zbuf[b, :, pl.ds(pl.multiple_of(r * ST, ST) + j * 128, 128)] = part
                x_t = x[j * 128:(j + 1) * 128, :].astype(F32).T
                st_ref[:, pl.ds(pl.multiple_of(r * ST, ST) + j * 128, 128)] = x_t.astype(BF16)

    col_part(0)
    col_send(0)
    v = col_wait(0)
    row_part(0, v, False)
    row_send(0)
    set_u(row_wait(0))
    col_part(1)
    col_send(1)
    v = col_wait(1)
    row_part(1, v, False)
    row_send(1)
    wait_bytes(sg.at[pl.ds(0, (NB - 1) * SB), :], s_rs)
    steps = SROWS // ST
    for step in range(steps // 2):
        student(step)
    set_u(row_wait(1))
    col_part(2)
    col_send(2)
    for step in range(steps // 2, steps):
        student(step)
    z_src = zbuf.at[b]
    b_all(lambda _: z_src, z_src, z_ss, z_rs)
    v = col_wait(2)
    row_part(2, v, True)
    row_send(2)
    b_all(lambda b2: hb.at[rows(b2, TB), :], hr.at[b], h_ss, h_rs)
    b_all(lambda b2: gb.at[rows(b2, SB), :], gr.at[b], g_ss, g_rs)

    wait_bytes(zbuf.at[pl.ds(0, NB - 1)], z_rs)
    zsum = zbuf[0]
    for i in range(1, NB):
        zsum = zsum + zbuf[i]
    ztmp[...] = zsum
    z_inv = 1.0 / zsum
    for j in range(SROWS // 512):
        szt[:, j * 512:(j + 1) * 512] = (
            st_ref[:, j * 512:(j + 1) * 512].astype(F32) * z_inv[:, j * 512:(j + 1) * 512]
        ).astype(BF16)

    @pl.loop(0, NA)
    def _(i):
        gw[i] = dot(szt[...], e3[i])

    u_row = row_wait(2)
    set_u(u_row)
    ua = []
    for j in range(TROWS // 128):
        mixed_t = dot(st_ref[:, j * 512:(j + 1) * 512], mix_big_ref[...])
        ua.append(mixed_t * u_row[:, j * 128:(j + 1) * 128])
    ua = jnp.concatenate(ua, axis=1)
    ua_high = ua.astype(BF16)
    ua = jnp.concatenate([ua_high, (ua - ua_high.astype(F32)).astype(BF16)], axis=0)

    def teacher_part(i):
        both = dot(ua, kv[i])
        return both[:D] + both[D:]

    for y2 in range(NY):
        i = y2 * 2 + 1 - c
        cs[y2] = gw[i] - teacher_part(i)
        remote(cs.at[y2], cr.at[y2], c_ss.at[y2], c_rs.at[y2], (dp, 1 - c)).start()
    for y2 in range(NY):
        i = y2 * 2 + c
        gw[i] = gw[i] - teacher_part(i)
    for o in list(range(1, NY)) + [0]:
        y2 = (y + o) % NY
        i = y2 * 2 + c
        wait_bytes(cr.at[y2], c_rs.at[y2])
        both = gw[i] + cr[y2]
        if o:
            ys[o - 1] = both.astype(BF16)
            remote(ys.at[o - 1], yr.at[o - 1], y_ss.at[o - 1], y_rs.at[o - 1],
                   (y2 * NB + b, c)).start()
        else:
            gw[i] = both

    hr[b] = hb[rows(b, TB), :]
    gr[b] = gb[rows(b, SB), :]
    wait_bytes(hr.at[pl.ds(0, NB - 1)], h_rs)
    h = jnp.zeros((TB, D), F32)
    for i in range(NB):
        h = h + hr[i].astype(F32)
    u_own = ub[rows(b, TB), :]
    mixed = dot(mix_ref[...], h * jnp.concatenate([u_own, u_own], axis=1),
                precision=lax.Precision.HIGHEST)
    wait_bytes(gr.at[pl.ds(0, NB - 1)], g_rs)
    g = lax.fori_loop(0, NB, lambda i, t: t + gr[i].astype(F32), jnp.zeros((SB, D), F32))
    ub[0:128, :] = column(ztmp[:, rows(b // 2, 128)])
    z_own = ub[rows(b % 2, SB), :]
    student_f = s_raw / snorm
    student_b = student_f.astype(BF16).astype(F32)
    grad_n = (g / jnp.concatenate([z_own, z_own], axis=1) - mixed) / student_temp
    loss = jnp.log(z_own) - jnp.sum(student_b * mixed, axis=1, keepdims=True) / student_temp
    grad_s = (grad_n - student_f * jnp.sum(student_f * grad_n, axis=1, keepdims=True)) / snorm
    out_ref[c, :, 0:D] = grad_s
    out_ref[c, :, D:] = loss
    out_copy = remote(out_ref.at[c], out_ref.at[c], o_ss, o_rs, (dp, 1 - c))
    out_copy.start()

    grad_w = gw[a]
    for o in range(1, NY):
        wait_bytes(yr.at[o - 1], y_rs.at[o - 1])
        grad_w = grad_w + yr[o - 1].astype(F32)
    grad_w = grad_w / student_temp
    weight_f = proto_f / colnorm
    gv_ref[...] = (
        grad_w - weight_f * jnp.sum(weight_f * grad_w, axis=0, keepdims=True)
    ) / colnorm

    wait_bytes(out_ref.at[1 - c], o_rs)
    out_copy.wait_send()
    for cp in w_copies:
        cp.wait_send()
    wait_bytes(tg.at[pl.ds(0, (NB - 1) * TB), :], t_ss)
    wait_bytes(sg.at[pl.ds(0, (NB - 1) * SB), :], s_ss)
    for sweep in range(SWEEPS):
        wait_bytes(colbuf.at[sweep, pl.ds(0, NA - 1)], col_ss.at[sweep])
        wait_bytes(rowbuf.at[sweep, pl.ds(0, NB - 1)], row_ss.at[sweep])
    wait_bytes(zbuf.at[pl.ds(0, NB - 1)], z_ss)
    wait_bytes(gr.at[pl.ds(0, NB - 1)], g_ss)
    wait_bytes(hr.at[pl.ds(0, NB - 1)], h_ss)
    for y2 in range(NY):
        wait_bytes(cs.at[y2], c_ss.at[y2])
    for o in range(1, NY):
        wait_bytes(ys.at[o - 1], y_ss.at[o - 1])


def shards(teacher_feats, student_feats, proto_v):
    c = lax.axis_index("proto")
    t = lax.dynamic_slice_in_dim(teacher_feats, c * IMG, IMG, 0).reshape(IMG * TEACH, D)
    s = lax.dynamic_slice_in_dim(student_feats, c * IMG, IMG, 0).reshape(IMG * CROPS, D)
    t = jnp.pad(t, ((0, TB - IMG * TEACH), (0, 0)))
    s = jnp.pad(s, ((0, SB - IMG * CROPS), (0, 0)))
    mix = mixing()
    mix_big = jnp.asarray(np.kron(np.eye(8, dtype=np.float32), mix), BF16)
    vmem = pl.BlockSpec(memory_space=pltpu.VMEM)
    dma = pltpu.SemaphoreType.DMA
    out, grad_v = pl.pallas_call(
        kernel,
        out_shape=(
            jax.ShapeDtypeStruct((2, SB, OUTW), F32),
            jax.ShapeDtypeStruct((D, PB), F32),
        ),
        in_specs=[vmem] * 5,
        out_specs=(vmem, vmem),
        scratch_shapes=[
            pltpu.VMEM((NA, D, PB), BF16),
            pltpu.VMEM((TROWS, D), BF16),
            pltpu.VMEM((SROWS, D), BF16),
            pltpu.VMEM((NA, TROWS, PB), F32),
            pltpu.VMEM((NA, TROWS, PB), BF16),
            pltpu.VMEM((NA, SROWS, PB), BF16),
            pltpu.VMEM((D, SROWS), BF16),
            pltpu.VMEM((D, SROWS), BF16),
            pltpu.VMEM((TROWS, 128), F32),
            pltpu.VMEM((SROWS, D), BF16),
            pltpu.VMEM((NB, SB, D), BF16),
            pltpu.VMEM((TROWS, D), BF16),
            pltpu.VMEM((NB, TB, D), BF16),
            pltpu.VMEM((NA, D, PB), F32),
            pltpu.VMEM((NY, D, PB), F32),
            pltpu.VMEM((NY, D, PB), F32),
            pltpu.VMEM((NY - 1, D, PB), BF16),
            pltpu.VMEM((NY - 1, D, PB), BF16),
            pltpu.VMEM((SWEEPS, NA, 1, NA * PB), F32),
            pltpu.VMEM((SWEEPS, NB, 1, TROWS), F32),
            pltpu.VMEM((NB, 1, SROWS), F32),
            pltpu.VMEM((1, SROWS), F32),
            dma((2 * NY - 1,)), dma((NA,)),
            dma, dma, dma, dma,
            dma((SWEEPS,)), dma((SWEEPS,)), dma((SWEEPS,)), dma((SWEEPS,)),
            dma, dma, dma, dma, dma, dma,
            dma((NY,)), dma((NY,)),
            dma((NY - 1,)), dma((NY - 1,)),
            dma, dma,
        ],
        compiler_params=pltpu.CompilerParams(
            collective_id=0, has_side_effects=True, vmem_limit_bytes=56 << 20
        ),
        name="head_step",
    )(t, s, proto_v, mix_big, jnp.asarray(mix))
    out = out[:, : IMG * CROPS, :].reshape(2 * IMG, CROPS, OUTW)
    return (out[:, :, D], out[:, :, :D], grad_v)


def solution(mesh):
    in_specs = (P("dp", None, None), P("dp", None, None), P(None, ("dp", "proto")))
    out_specs = (P("dp", None), P("dp", None, None), P(None, ("dp", "proto")))
    return jax.shard_map(shards, mesh=mesh, in_specs=in_specs, out_specs=out_specs, check_vma=False)
```

time: 1500 us -> 107 us (0.07)
  blocking collectives: 842 us -> 0 us
  waiting for transfers between devices: 512 us -> 0 us
  Pallas kernels: 0 us -> 101 us
  local copies, waits for them, and re-layouts: 57.1 us -> 5.35 us
  other arithmetic: 44.1 us -> 0 us
  matrix products: 29.5 us -> 0 us
    unnamed x1 -> x0, blocking collectives: 578 us -> none
    psum x2 -> x0, waiting for transfers between devices: 281 us -> none  [the longest x1 249 us: shards(): row_total = lax.psum(jnp.sum(targets, axis=1), ('dp', 'proto'))]
    psum x3 -> x0, blocking collectives: 264 us -> none  [the longest x2 153 us: shards(): row_total = lax.psum(jnp.sum(targets, axis=1), ('dp', 'proto'))]
    reduce_scatter x1 -> x0, waiting for transfers between devices: 128 us -> none  [shards(): lax.psum_scatter(grad_part, 'dp', scatter_dimension=0, tiled=True)]
    all_gather x2 -> x0, waiting for transfers between devices: 102 us -> none  [the longest x1 102 us: shards(): lax.all_gather(teacher_n, 'dp', axis=0, tiled=True)]
    pallas_call x0 -> x1, Pallas kernels: none -> 101 us  [shards(): pl.pallas_call(kernel, out_shape=(jax.ShapeDtypeStruct((2, SB, OUTW), F32...]
    concatenate x2 -> x0, local copies, waits for them, and re-layouts: 37 us -> none  [targets_mix(): jnp.concatenate([second_crop[:, None, :], first_crop[:, None, :], locals_...]
    dot_general x4 -> x0, matrix products: 29.5 us -> none  [the longest x1 11.8 us: shards(): jnp.dot(every_student, weight_b, preferred_element_type=jnp.float32)]
  transfers between devices with their start and end apart: 5 -> 0, of which waited for: 4 -> 0; matrix products, arithmetic and copies ran while one was open for 1% -> 0% of each run, Pallas kernels for 0% -> 0%
where the time goes in v1:
time: 107 us
  Pallas kernels  101 us (94%)
  local copies, waits for them, and re-layouts  5.35 us (5%)
    pallas_call x1, Pallas kernels, shards(): pl.pallas_call(kernel, out_shape=(jax.ShapeDtypeStruct((2, SB, OUTW), F32...  101 us
    unnamed x8, local copies, waits for them, and re-layouts  2.38 us

profile of v1, /device:TPU:1, one launch (start us, length us, event | category | flops | bytes accessed | tf_op | source)
XLA Modules:
  0.0 107.1 jit_solution(9966443760004057634)
XLA Ops:
  0.6 0.0 copy-start
  0.6 0.0 copy-start.2
  0.7 0.7 copy-done.2
  1.4 0.6 pad.8.t_ref
  2.0 0.0 copy-done
  2.1 0.6 pad.9.s_ref
  2.7 101.1 %head_step.1 = (f32[2,64,384]{2,1,0:T(8,128)}, f32[256,256]{1,0:T(8,128)}) custom-call(bf16[16,256]{1,0:T(8,128)(2,1)} %pad.8.t_ref, bf16[64,256]{1,0:T(8,128)(2,1)} %pad.9.s_ref, bf16[256,256]{1,0:T(8,128)(2,1)} %p_ref.1, bf16[512,128]{1,0:T(8,128)(2,1)} %constant.16.clone.mix_big_ref, f32[64,16]{1,0:T(8,128)} %constant.17.clone.mix_ref), custom_call_target="tpu_custom_call" | custom-call | tf_op jit(solution)/shard_map/head_step/pallas_call | solution.py:355
  103.8 1.0 reshape.17
  104.8 0.7 slice_reduce_fusion
  105.5 0.0 copy-start.1
  105.5 0.7 copy.14
  106.2 0.2 copy-done.1
  106.4 0.7 copy.16
  (6 shorter events, 0.1 us)
Async XLA Ops:
  0.6 1.4 %copy-start = (bf16[12,10,256]{2,0,1:T(8,128)(2,1)S(1)}, bf16[12,10,256]{2,0,1:T(8,128)(2,1)}, u32[]{:S(2)}) copy-start(bf16[12,10,256]{2,0,1:T(8,128)(2,1)} %param.6) | copy-start | bytes 184324
  0.6 0.7 copy-start.2
  105.5 1.0 copy-start.1

commit v2 on v1

v2 whole, which is shorter than its diff:
```python
import math

import jax
import jax.numpy as jnp
import numpy as np
from jax import lax
from jax.experimental import pallas as pl
from jax.experimental.pallas import tpu as pltpu
from jax.sharding import PartitionSpec as P

MESH = pl.DeviceIdType.MESH
F32, BF16 = jnp.float32, jnp.bfloat16

epsilon = 1e-12
teacher_temp = 0.07
student_temp = 0.1
LOG2E = math.log2(math.e)

NY, NX, NZ = 4, 4, 8
NB, NA = NX * NZ, NY * 2
D = 256
PB = 256
SB, TB = 64, 16
SROWS, TROWS = SB * NB, TB * NB
IMG, CROPS, TEACH = 6, 10, 2
SWEEPS = 3
ST = SB * NZ
OUTW = D + 128


def mixing():
    m = np.zeros((SB, TB), np.float32)
    for img in range(IMG):
        for crop in range(CROPS):
            row, first = crop * IMG + img, img * TEACH
            if crop == 0:
                m[row, first + 1] = 1.0
            elif crop == 1:
                m[row, first] = 1.0
            else:
                m[row, first] = m[row, first + 1] = 0.5
    return m


def dot(x, y, dims=((1,), (0,)), precision=None):
    return lax.dot_general(x, y, (dims, ((), ())), preferred_element_type=F32, precision=precision)


def wait_bytes(ref, sem):
    pltpu.make_async_copy(ref, ref, sem).wait()


def column(row):
    return jnp.broadcast_to(row, (128, 128)).T


def kernel(t_ref, s_ref, p_ref, mix_big_ref, mix_ref, out_ref, gv_ref,
           wg, tg, sg, k3, kv, e3, st_ref, szt, ub, gb, gs, gx, gz, gr, hb, hx, hz, hr, gw, cs, cr, ys, yr,
           colbuf, rowbuf, zx, zbuf, zown, ztmp, ztot, traw, sraw, at, ats, kvs, uu,
           w_ss, w_rs, t_ss, t_rs, sz_ss, sz_rs, sx_ss, sx_rs, gx_ss, gx_rs, col_ss, col_rs, row_ss, row_rs, z_ss, z_rs,
           g_ss, g_rs, h_ss, h_rs, c_ss, c_rs, y_ss, y_rs, o_ss, o_rs,
           k_ss, k_rs, at_ss, at_rs, u_ss, u_rs, zx_ss, zx_rs, hx_ss, hx_rs):
    dp = lax.axis_index("dp")
    c = lax.axis_index("proto")
    y, b = dp // NB, dp % NB
    x, zz = b // NZ, b % NZ
    a = y * 2 + c

    def a_dev(a2):
        return ((a2 // 2) * NB + b, a2 % 2)

    def b_dev(b2):
        return (y * NB + b2, c)

    def a_peer(o):
        return (a + o) % NA

    def x_peer(o):
        return (x + o) % NX

    def z_peer(o):
        return (zz + o) % NZ

    def far(i, n):
        return (n // 2 + (2 * (i % 2) - 1) * ((i + 1) // 2)) % n

    def b_far(i):
        return x_peer(far(i % NX, NX)) * NZ + z_peer(far(i // NX, NZ))

    def rows(i, n):
        return pl.ds(pl.multiple_of(i * n, n), n)

    def remote(src, dst, ss, rs, device):
        return pltpu.make_async_remote_copy(
            src_ref=src, dst_ref=dst, send_sem=ss, recv_sem=rs, device_id=device, device_id_type=MESH
        )

    comms = {
        "t": (tg.at[pl.ds(0, (NB - 1) * TB), :], t_ss, t_rs),
        "at": (at, at_ss, at_rs),
        "u": (uu.at[0], u_ss, u_rs),
        "zx": (zx, zx_ss, zx_rs),
        "z": (zbuf, z_ss, z_rs),
        "hx": (hx, hx_ss, hx_rs),
        "g": (gr.at[pl.ds(0, NZ - 1)], g_ss, g_rs),
        "h": (hr, h_ss, h_rs),
    }
    for sweep in range(SWEEPS):
        comms["col%d" % sweep] = (colbuf.at[sweep, pl.ds(0, NA - 1)], col_ss.at[sweep], col_rs.at[sweep])
        comms["row%d" % sweep] = (rowbuf.at[sweep, pl.ds(0, NB - 1)], row_ss.at[sweep], row_rs.at[sweep])
    for z2 in range(1, NZ):
        comms["sz%d" % z2] = (sg.at[pl.ds(0, SB), :], sz_ss.at[z2 - 1], sz_rs.at[z2 - 1])
    for o in range(1, NX):
        comms["sx%d" % o] = (sg.at[pl.ds(0, NZ * SB), :], sx_ss.at[o - 1], sx_rs.at[o - 1])
        comms["gx%d" % o] = (gx.at[o - 1], gx_ss.at[o - 1], gx_rs.at[o - 1])
    for y2 in range(NY):
        comms["c%d" % y2] = (cs.at[y2], c_ss.at[y2], c_rs.at[y2])
        comms["k%d" % y2] = (kvs.at[y2], k_ss.at[y2], k_rs.at[y2])
    for o in range(NY - 1):
        comms["y%d" % o] = (ys.at[o], y_ss.at[o], y_rs.at[o])
    started, received = [], set()

    def recv(name):
        wait_bytes(comms[name][0], comms[name][2])
        received.add(name)

    def finish():
        for name in started:
            if name not in received:
                recv(name)
            wait_bytes(comms[name][0], comms[name][1])
        for cp in w_copies:
            cp.wait_send()

    barrier = pltpu.get_barrier_semaphore()

    @pl.loop(0, NB - 1)
    def _(i):
        pl.semaphore_signal(barrier, inc=1, device_id=b_dev(b_far(i)), device_id_type=MESH)

    @pl.loop(1, NA)
    def _(o):
        pl.semaphore_signal(barrier, inc=1, device_id=a_dev(a_peer(o)), device_id_type=MESH)

    proto_f = p_ref[...].astype(F32)
    colnorm = jnp.sqrt(jnp.sum(proto_f * proto_f, axis=0, keepdims=True) + epsilon)
    wg[a] = (proto_f / colnorm).astype(BF16)
    traw[...] = jnp.zeros_like(traw)
    for img in range(IMG):
        traw[img * TEACH:(img + 1) * TEACH, :] = t_ref[c * IMG + img].astype(F32)
    t_f = traw[...]
    tg[rows(b, TB), :] = (
        t_f / jnp.sqrt(jnp.sum(t_f * t_f, axis=1, keepdims=True) + epsilon)
    ).astype(BF16)
    sraw[...] = jnp.zeros_like(sraw)
    for crop in range(CROPS):
        both = s_ref[crop].astype(F32)
        sraw[crop * IMG:(crop + 1) * IMG, :] = jnp.where(c == 0, both[:IMG], both[IMG:])
    s_raw = sraw[...]
    snorm = jnp.sqrt(jnp.sum(s_raw * s_raw, axis=1, keepdims=True) + epsilon)
    sg[rows(b, SB), :] = (s_raw / snorm).astype(BF16)

    pl.semaphore_wait(barrier, NA - 1 + NB - 1)

    w_copies = []
    for o in (2, 1, 3):
        cp = remote(wg.at[a], wg.at[a], w_ss.at[o - 1], w_rs.at[a], a_dev(a_peer(2 * o)))
        cp.start()
        w_copies.append(cp)

    def b_all(name, src, dst):
        started.append(name)
        _, ss, rs = comms[name]

        @pl.loop(0, NB - 1)
        def _(i):
            b2 = b_far(i)
            remote(src(b2), dst, ss, rs, b_dev(b2)).start()

    def to_sibling(name, src, dst):
        started.append(name)
        remote(src, dst, comms[name][1], comms[name][2], (dp, 1 - c)).start()

    t_own = tg.at[rows(b, TB), :]
    b_all("t", lambda _: t_own, t_own)
    cp = remote(wg.at[a], wg.at[a], w_ss.at[NY - 1], w_rs.at[a], (dp, 1 - c))
    cp.start()
    w_copies.append(cp)
    s_own = sg.at[rows(b, SB), :]

    def s_forward(z2):
        src = sg.at[rows(x * NZ + z2, SB), :]
        for o in range(1, NX):
            remote(src, src, sx_ss.at[o - 1], sx_rs.at[o - 1], b_dev(x_peer(o) * NZ + zz)).start()

    z_order = [1, 7, 2, 6, 3, 5, 4]
    for o in z_order:
        started.append("sz%d" % o)
        remote(s_own, s_own, sz_ss.at[o - 1], sz_rs.at[o - 1], b_dev(x * NZ + z_peer(o))).start()
    for o in range(1, NX):
        started.append("sx%d" % o)
    s_forward(zz)

    for o in range(1, NY):
        a2 = a_peer(2 * (NY - o))
        wait_bytes(wg.at[a2], w_rs.at[a2])
        cp = remote(wg.at[a2], wg.at[a2], w_ss.at[NY - 1 + o], w_rs.at[a2], (dp, 1 - c))
        cp.start()
        w_copies.append(cp)
    for o in (7, 1, 6, 2, 5, 3, 4):
        recv("sz%d" % o)
        s_forward(z_peer(NZ - o))
    for y2 in range(NY):
        a2 = y2 * 2 + 1 - c
        wait_bytes(wg.at[a2], w_rs.at[a2])
    recv("t")

    valid = (lax.broadcasted_iota(jnp.int32, (1, TROWS), 1) % TB < IMG * TEACH).astype(F32)

    def set_u(u_row):
        for r in range(TROWS // 128):
            ub[r * 128:(r + 1) * 128, :] = column(u_row[:, r * 128:(r + 1) * 128])

    set_u(valid)

    def col_send(sweep):
        src = colbuf.at[sweep, a]
        started.append("col%d" % sweep)

        @pl.loop(1, NA)
        def _(o):
            remote(src, src, col_ss.at[sweep], col_rs.at[sweep], a_dev(a_peer(o))).start()

    def col_wait(sweep):
        recv("col%d" % sweep)
        total = colbuf[sweep, 0]
        for i in range(1, NA):
            total = total + colbuf[sweep, i]
        return 1.0 / total

    def row_send(sweep):
        src = rowbuf.at[sweep, b]
        b_all("row%d" % sweep, lambda _: src, src)

    def row_wait(sweep):
        recv("row%d" % sweep)
        total = rowbuf[sweep, 0]
        for i in range(1, NB):
            total = total + rowbuf[sweep, i]
        return valid / total

    def col_part(sweep):
        @pl.loop(0, NA)
        def _(i):
            u2 = ub[...]
            part = jnp.sum(k3[i] * jnp.concatenate([u2, u2], axis=1), axis=0, keepdims=True)
            colbuf[sweep, a, :, rows(i, PB)] = part

    def row_part(sweep, v, last):
        @pl.loop(0, TROWS // 128)
        def _(r):
            acc = jnp.zeros((128, 128), F32)
            h = jnp.zeros((128, D), F32)
            for i in range(NA):
                scaled = k3[i, rows(r, 128), :] * v[:, i * PB:(i + 1) * PB]
                acc = acc + scaled[:, :128] + scaled[:, 128:]
                if last:
                    scaled = scaled.astype(BF16)
                    kv[i, rows(r, 128), :] = scaled
                    h = h + dot(scaled, wg[i], ((1,), (1,)))
            rowbuf[sweep, b, :, rows(r, 128)] = jnp.sum(acc.T, axis=0, keepdims=True)
            if last:
                hb[rows(r, 128), :] = h.astype(BF16)

    @pl.loop(0, NA)
    def _(i):
        k3[i] = jnp.exp2(dot(tg[...], wg[i]) * (LOG2E / teacher_temp))

    def student(step):
        @pl.loop(step, step + 1)
        def _(step):
            r = x_peer(NX - step)
            feats = sg[rows(r, ST), :]
            z = jnp.zeros((ST, 128), F32)
            g = jnp.zeros((ST, D), F32)
            for i in range(NA):
                e = jnp.exp2(dot(feats, wg[i]) * (LOG2E / student_temp))
                z = z + e[:, :128] + e[:, 128:]
                e = e.astype(BF16)
                e3[i, rows(r, ST), :] = e
                g = g + dot(e, wg[i], ((1,), (1,)))
            gb[step] = g
            for j in range(ST // 128):
                part = jnp.sum(z[j * 128:(j + 1) * 128, :].T, axis=0, keepdims=True)
                zown[:, pl.ds(pl.multiple_of(r * ST, ST) + j * 128, 128)] = part
                f_t = feats[j * 128:(j + 1) * 128, :].astype(F32).T
                st_ref[:, pl.ds(pl.multiple_of(r * ST, ST) + j * 128, 128)] = f_t.astype(BF16)

    def student_send(step):
        if step:
            o = NX - step
            gs[step - 1] = gb[step].astype(BF16)
            started.append("gx%d" % o)
            remote(gs.at[step - 1], gx.at[o - 1], gx_ss.at[o - 1], gx_rs.at[o - 1],
                   b_dev(x_peer(o) * NZ + zz)).start()

    def student_step(step):
        if step:
            recv("sx%d" % step)
        student(step)

    col_part(0)
    col_send(0)
    student_step(0)
    v = col_wait(0)
    row_part(0, v, False)
    row_send(0)
    student_step(1)
    student_step(3)
    set_u(row_wait(0))
    col_part(1)
    col_send(1)
    student_send(1)
    student_send(3)
    student_step(2)
    started.append("zx")
    for o in range(1, NX):
        remote(zown, zx.at[o - 1], zx_ss, zx_rs, b_dev(x_peer(o) * NZ + zz)).start()
    v = col_wait(1)
    row_part(1, v, False)
    row_send(1)
    recv("zx")
    ztmp[...] = zown[...] + zx[0] + zx[1] + zx[2]
    set_u(row_wait(1))
    col_part(2)
    col_send(2)
    student_send(2)
    started.append("z")
    for o in z_order:
        remote(ztmp, zbuf.at[o - 1], z_ss, z_rs, b_dev(x * NZ + z_peer(o))).start()
    for j in range(TROWS // 128):
        at[:, j * 128:(j + 1) * 128] = dot(st_ref[:, j * 512:(j + 1) * 512], mix_big_ref[...])
    to_sibling("at", at, ats)
    v = col_wait(2)
    row_part(2, v, True)
    row_send(2)
    started.append("hx")
    for o in range(1, NX):
        remote(hb.at[rows(x_peer(o), NZ * TB), :], hx.at[o - 1], hx_ss, hx_rs,
               b_dev(x_peer(o) * NZ + zz)).start()
    for y2 in range(NY):
        to_sibling("k%d" % y2, kv.at[y2 * 2 + 1 - c], kvs.at[y2])
    recv("z")
    zsum = ztmp[...]
    for i in range(NZ - 1):
        zsum = zsum + zbuf[i]
    ztot[...] = zsum
    z_inv = 1.0 / zsum
    for j in range(SROWS // 512):
        szt[:, j * 512:(j + 1) * 512] = (
            st_ref[:, j * 512:(j + 1) * 512].astype(F32) * z_inv[:, j * 512:(j + 1) * 512]
        ).astype(BF16)
    for y2 in range(NY):
        cs[y2] = dot(szt[...], e3[y2 * 2 + 1 - c])
        to_sibling("c%d" % y2, cs.at[y2], cr.at[y2])
    for y2 in range(NY):
        gw[y2] = dot(szt[...], e3[y2 * 2 + c])
    for o in range(1, NX):
        recv("gx%d" % o)
    started.append("g")
    for o in z_order + [0]:
        z2 = z_peer(o)
        g = gb[0, rows(z2, SB), :]
        for i in range(NX - 1):
            g = g + gx[i, rows(z2, SB), :].astype(F32)
        gz[o] = g.astype(BF16)
        if o:
            remote(gz.at[o], gr.at[o - 1], g_ss, g_rs, b_dev(x * NZ + z2)).start()
    u_row = row_wait(2)
    uu[c] = u_row
    to_sibling("u", uu.at[c], uu.at[c])
    recv("hx")
    started.append("h")
    for o in z_order + [0]:
        z2 = z_peer(o)
        h = hb[rows(x * NZ + z2, TB), :].astype(F32)
        for i in range(NX - 1):
            h = h + hx[i, rows(z2, TB), :].astype(F32)
        hz[o] = h.astype(BF16)
        if o:
            remote(hz.at[o], hr.at[o - 1], h_ss, h_rs, b_dev(x * NZ + z2)).start()
    set_u(u_row)

    def scaled_mix(mixed_t, u2):
        full = mixed_t * u2
        high = full.astype(BF16)
        return jnp.concatenate([high, (full - high.astype(F32)).astype(BF16)], axis=0)

    def teacher_part(ua, k2):
        both = dot(ua, k2)
        return both[:D] + both[D:]

    ua = scaled_mix(at[...], u_row)
    for y2 in range(NY):
        gw[y2] = gw[y2] - teacher_part(ua, kv[y2 * 2 + c])
    recv("at")
    recv("u")
    ua = scaled_mix(ats[...], uu[1 - c])
    for name in range(NY):
        recv("k%d" % name)
        recv("c%d" % name)
    for o in (2, 1, 3, 0):
        y2 = (y + o) % NY
        both = gw[y2] + cr[y2] - teacher_part(ua, kvs[y2])
        if o:
            ys[o - 1] = both.astype(BF16)
            started.append("y%d" % (o - 1))
            remote(ys.at[o - 1], yr.at[o - 1], y_ss.at[o - 1], y_rs.at[o - 1],
                   (y2 * NB + b, c)).start()
        else:
            gw[y2] = both

    recv("h")
    h = hz[0].astype(F32)
    for i in range(NZ - 1):
        h = h + hr[i].astype(F32)
    u_own = ub[rows(b, TB), :]
    mixed = dot(mix_ref[...], h * jnp.concatenate([u_own, u_own], axis=1),
                precision=lax.Precision.HIGHEST)
    recv("g")
    g = gz[0].astype(F32)
    for i in range(NZ - 1):
        g = g + gr[i].astype(F32)
    ub[0:128, :] = column(ztot[:, rows(b // 2, 128)])
    z_own = ub[rows(b % 2, SB), :]
    student_f = s_raw / snorm
    student_b = student_f.astype(BF16).astype(F32)
    grad_n = (g / jnp.concatenate([z_own, z_own], axis=1) - mixed) / student_temp
    loss = jnp.log(z_own) - jnp.sum(student_b * mixed, axis=1, keepdims=True) / student_temp
    grad_s = (grad_n - student_f * jnp.sum(student_f * grad_n, axis=1, keepdims=True)) / snorm
    out_ref[c, :, 0:D] = grad_s
    out_ref[c, :, D:] = loss
    out_copy = remote(out_ref.at[c], out_ref.at[c], o_ss, o_rs, (dp, 1 - c))
    out_copy.start()

    grad_w = gw[y]
    for o in range(1, NY):
        recv("y%d" % (o - 1))
        grad_w = grad_w + yr[o - 1].astype(F32)
    grad_w = grad_w / student_temp
    weight_f = proto_f / colnorm
    gv_ref[...] = (
        grad_w - weight_f * jnp.sum(weight_f * grad_w, axis=0, keepdims=True)
    ) / colnorm

    wait_bytes(out_ref.at[1 - c], o_rs)
    out_copy.wait_send()
    finish()


def write_out(out_ref, gv_ref, loss_ref, gs_ref, gw_ref):
    gw_ref[...] = gv_ref[...]
    lane = lax.broadcasted_iota(jnp.int32, (IMG, OUTW - D), 1)
    for half in range(2):
        images = slice(half * IMG, (half + 1) * IMG)
        loss = jnp.zeros((IMG, OUTW - D), F32)
        for crop in range(CROPS):
            rows = slice(crop * IMG, (crop + 1) * IMG)
            gs_ref[crop, images, :] = out_ref[half, rows, 0:D]
            loss = jnp.where(lane == crop, out_ref[half, rows, D:], loss)
        loss_ref[images, :] = loss[:, 0:CROPS]


def shards(teacher_feats, student_feats, proto_v):
    mix = mixing()
    mix_big = jnp.asarray(np.kron(np.eye(8, dtype=np.float32), mix), BF16)
    vmem = pl.BlockSpec(memory_space=pltpu.VMEM)
    dma = pltpu.SemaphoreType.DMA
    out, grad_v = pl.pallas_call(
        kernel,
        out_shape=(
            jax.ShapeDtypeStruct((2, SB, OUTW), F32),
            jax.ShapeDtypeStruct((D, PB), F32),
        ),
        in_specs=[vmem] * 5,
        out_specs=(vmem, vmem),
        scratch_shapes=[
            pltpu.VMEM((NA, D, PB), BF16),
            pltpu.VMEM((TROWS, D), BF16),
            pltpu.VMEM((SROWS, D), BF16),
            pltpu.VMEM((NA, TROWS, PB), F32),
            pltpu.VMEM((NA, TROWS, PB), BF16),
            pltpu.VMEM((NA, SROWS, PB), BF16),
            pltpu.VMEM((D, SROWS), BF16),
            pltpu.VMEM((D, SROWS), BF16),
            pltpu.VMEM((TROWS, 128), F32),
            pltpu.VMEM((NX, ST, D), F32),
            pltpu.VMEM((NX - 1, ST, D), BF16),
            pltpu.VMEM((NX - 1, ST, D), BF16),
            pltpu.VMEM((NZ, SB, D), BF16),
            pltpu.VMEM((NZ - 1, SB, D), BF16),
            pltpu.VMEM((TROWS, D), BF16),
            pltpu.VMEM((NX - 1, NZ * TB, D), BF16),
            pltpu.VMEM((NZ, TB, D), BF16),
            pltpu.VMEM((NZ - 1, TB, D), BF16),
            pltpu.VMEM((NY, D, PB), F32),
            pltpu.VMEM((NY, D, PB), F32),
            pltpu.VMEM((NY, D, PB), F32),
            pltpu.VMEM((NY - 1, D, PB), BF16),
            pltpu.VMEM((NY - 1, D, PB), BF16),
            pltpu.VMEM((SWEEPS, NA, 1, NA * PB), F32),
            pltpu.VMEM((SWEEPS, NB, 1, TROWS), F32),
            pltpu.VMEM((NX - 1, 1, SROWS), F32),
            pltpu.VMEM((NZ - 1, 1, SROWS), F32),
            pltpu.VMEM((1, SROWS), F32),
            pltpu.VMEM((1, SROWS), F32),
            pltpu.VMEM((1, SROWS), F32),
            pltpu.VMEM((TB, D), F32),
            pltpu.VMEM((SB, D), F32),
            pltpu.VMEM((D, TROWS), F32),
            pltpu.VMEM((D, TROWS), F32),
            pltpu.VMEM((NY, TROWS, PB), BF16),
            pltpu.VMEM((2, 1, TROWS), F32),
            dma((2 * NY - 1,)), dma((NA,)),
            dma, dma,
            dma((NZ - 1,)), dma((NZ - 1,)), dma((NX - 1,)), dma((NX - 1,)),
            dma((NX - 1,)), dma((NX - 1,)),
            dma((SWEEPS,)), dma((SWEEPS,)), dma((SWEEPS,)), dma((SWEEPS,)),
            dma, dma, dma, dma, dma, dma,
            dma((NY,)), dma((NY,)),
            dma((NY - 1,)), dma((NY - 1,)),
            dma, dma,
            dma((NY,)), dma((NY,)),
            dma, dma, dma, dma,
            dma, dma, dma, dma,
        ],
        compiler_params=pltpu.CompilerParams(
            collective_id=0, has_side_effects=True, vmem_limit_bytes=56 << 20
        ),
        name="head_step",
    )(teacher_feats, jnp.transpose(student_feats, (1, 0, 2)), proto_v, mix_big, jnp.asarray(mix))
    loss, grad_s, grad_v = pl.pallas_call(
        write_out,
        out_shape=(
            jax.ShapeDtypeStruct((2 * IMG, CROPS), F32),
            jax.ShapeDtypeStruct((CROPS, 2 * IMG, D), F32),
            jax.ShapeDtypeStruct((D, PB), F32),
        ),
        in_specs=[vmem] * 2,
        out_specs=(vmem,) * 3,
        name="write_out",
    )(out, grad_v)
    return (loss, jnp.transpose(grad_s, (1, 0, 2)), grad_v)


def solution(mesh):
    in_specs = (P("dp", None, None), P("dp", None, None), P(None, ("dp", "proto")))
    out_specs = (P("dp", None), P("dp", None, None), P(None, ("dp", "proto")))
    return jax.shard_map(shards, mesh=mesh, in_specs=in_specs, out_specs=out_specs, check_vma=False)
```

time: 107 us -> 79.7 us (0.74)
  Pallas kernels: 101 us -> 79 us
  local copies, waits for them, and re-layouts: 5.35 us -> 0 us
    pallas_call x1, Pallas kernels: 101 us -> 77.1 us  [shards(): pl.pallas_call(kernel, out_shape=(jax.ShapeDtypeStruct((2, SB, OUTW), F32...]
    unnamed x8 -> x0, local copies, waits for them, and re-layouts: 2.38 us -> none
    pallas_call x0 -> x1, Pallas kernels: none -> 1.84 us  [shards(): pl.pallas_call(write_out, out_shape=(jax.ShapeDtypeStruct((2 * IMG, CROPS...]
    pad x2 -> x0, local copies, waits for them, and re-layouts: 1.23 us -> none  [the longest x1 0.62 us: shards(): s = jnp.pad(s, ((0, SB - IMG * CROPS), (0, 0)))]
where the time goes in v2:
time: 79.7 us; the launch traced here: 79.6 us
  Pallas kernels  79 us (99%)
    pallas_call x1, Pallas kernels, shards(): pl.pallas_call(kernel, out_shape=(jax.ShapeDtypeStruct((2, SB, OUTW), F32...  77.1 us
    pallas_call x1, Pallas kernels, shards(): pl.pallas_call(write_out, out_shape=(jax.ShapeDtypeStruct((2 * IMG, CROPS...  1.84 us

profile of v2, /device:TPU:1, one launch (start us, length us, event | category | flops | bytes accessed | tf_op | source)
XLA Modules:
  0.0 79.6 jit_solution(8880319039679138605)
XLA Ops:
  0.6 77.1 %head_step.1 = (f32[2,64,384]{2,1,0:T(8,128)}, f32[256,256]{1,0:T(8,128)}) custom-call(bf16[12,2,256]{2,1,0:T(2,128)(2,1)} %t_ref.1, bf16[10,12,256]{2,1,0:T(8,128)(2,1)} %bitcast.2, bf16[256,256]{1,0:T(8,128)(2,1)} %p_ref.1, bf16[512,128]{1,0:T(8,128)(2,1)} %constant.4.clone.mix_big_ref, f32[64,16]{1,0:T(8,128)} %constant.5.clone.mix_ref), custom_call_target="tpu_custom_call" | custom-call | tf_op jit(solution)/shard_map/head_step/pallas_call | solution.py:479
  77.8 1.8 %write_out.1 = (f32[12,10]{1,0:T(8,128)}, f32[10,12,256]{2,1,0:T(8,128)}, f32[256,256]{1,0:T(8,128)}) custom-call(f32[2,64,384]{2,1,0:T(8,128)} %get-tuple-element.8.out_ref, f32[256,256]{1,0:T(8,128)} %get-tuple-element.9.gv_ref), custom_call_target="tpu_custom_call" | custom-call | tf_op jit(solution)/shard_map/write_out/pallas_call | solution.py:542

commit v3 on v2

--- a/solution.py
+++ b/solution.py
@@ -54,7 +54,8 @@
     return jnp.broadcast_to(row, (128, 128)).T
 
 
-def kernel(t_ref, s_ref, p_ref, mix_big_ref, mix_ref, out_ref, gv_ref,
+def kernel(t_hbm, s_hbm, p_hbm, mix_big_hbm, mix_hbm, out_ref, gv_ref,
+           t_ref, s_ref, p_ref, mix_big_ref, mix_ref, in_sem,
            wg, tg, sg, k3, kv, e3, st_ref, szt, ub, gb, gs, gx, gz, gr, hb, hx, hz, hr, gw, cs, cr, ys, yr,
            colbuf, rowbuf, zx, zbuf, zown, ztmp, ztot, traw, sraw, at, ats, kvs, uu,
            w_ss, w_rs, t_ss, t_rs, sz_ss, sz_rs, sx_ss, sx_rs, gx_ss, gx_rs, col_ss, col_rs, row_ss, row_rs, z_ss, z_rs,
@@ -142,6 +143,16 @@
     def _(o):
         pl.semaphore_signal(barrier, inc=1, device_id=a_dev(a_peer(o)), device_id_type=MESH)
 
+    inputs = [
+        pltpu.make_async_copy(src, dst, in_sem.at[n])
+        for n, (src, dst) in enumerate([
+            (p_hbm, p_ref), (t_hbm, t_ref), (s_hbm, s_ref), (mix_big_hbm, mix_big_ref), (mix_hbm, mix_ref)])
+    ]
+    for cp in inputs:
+        cp.start()
+    for cp in inputs:
+        cp.wait()
+
     proto_f = p_ref[...].astype(F32)
     colnorm = jnp.sqrt(jnp.sum(proto_f * proto_f, axis=0, keepdims=True) + epsilon)
     wg[a] = (proto_f / colnorm).astype(BF16)
@@ -207,14 +218,13 @@
         cp = remote(wg.at[a2], wg.at[a2], w_ss.at[NY - 1 + o], w_rs.at[a2], (dp, 1 - c))
         cp.start()
         w_copies.append(cp)
-    for o in (7, 1, 6, 2, 5, 3, 4):
-        recv("sz%d" % o)
-        s_forward(z_peer(NZ - o))
-    for y2 in range(NY):
-        a2 = y2 * 2 + 1 - c
-        wait_bytes(wg.at[a2], w_rs.at[a2])
+    def s_on(offsets):
+        for o in offsets:
+            recv("sz%d" % o)
+            s_forward(z_peer(NZ - o))
+
+    s_on((7, 1, 6, 2))
     recv("t")
-
     valid = (lax.broadcasted_iota(jnp.int32, (1, TROWS), 1) % TB < IMG * TEACH).astype(F32)
 
     def set_u(u_row):
@@ -272,9 +282,12 @@
             if last:
                 hb[rows(r, 128), :] = h.astype(BF16)
 
-    @pl.loop(0, NA)
-    def _(i):
-        k3[i] = jnp.exp2(dot(tg[...], wg[i]) * (LOG2E / teacher_temp))
+    def targets(i):
+        k = jnp.exp2(dot(tg[...], wg[i]) * (LOG2E / teacher_temp))
+        k3[i] = k
+        u2 = ub[...]
+        colbuf[0, a, :, rows(i, PB)] = jnp.sum(
+            k * jnp.concatenate([u2, u2], axis=1), axis=0, keepdims=True)
 
     def student(step):
         @pl.loop(step, step + 1)
@@ -309,8 +322,15 @@
             recv("sx%d" % step)
         student(step)
 
-    col_part(0)
+    targets(a)
+    for o in range(1, NY):
+        targets(a_peer(2 * (NY - o)))
+    for o in (0, 3, 2, 1):
+        a2 = ((y + o) % NY) * 2 + 1 - c
+        wait_bytes(wg.at[a2], w_rs.at[a2])
+        targets(a2)
     col_send(0)
+    s_on((5, 3, 4))
     student_step(0)
     v = col_wait(0)
     row_part(0, v, False)
@@ -376,9 +396,6 @@
         gz[o] = g.astype(BF16)
         if o:
             remote(gz.at[o], gr.at[o - 1], g_ss, g_rs, b_dev(x * NZ + z2)).start()
-    u_row = row_wait(2)
-    uu[c] = u_row
-    to_sibling("u", uu.at[c], uu.at[c])
     recv("hx")
     started.append("h")
     for o in z_order + [0]:
@@ -389,6 +406,9 @@
         hz[o] = h.astype(BF16)
         if o:
             remote(hz.at[o], hr.at[o - 1], h_ss, h_rs, b_dev(x * NZ + z2)).start()
+    u_row = row_wait(2)
+    uu[c] = u_row
+    to_sibling("u", uu.at[c], uu.at[c])
     set_u(u_row)
 
     def scaled_mix(mixed_t, u2):
@@ -482,9 +502,15 @@
             jax.ShapeDtypeStruct((2, SB, OUTW), F32),
             jax.ShapeDtypeStruct((D, PB), F32),
         ),
-        in_specs=[vmem] * 5,
+        in_specs=[pl.BlockSpec(memory_space=pl.ANY)] * 5,
         out_specs=(vmem, vmem),
         scratch_shapes=[
+            pltpu.VMEM((2 * IMG, TEACH, D), BF16),
+            pltpu.VMEM((CROPS, 2 * IMG, D), BF16),
+            pltpu.VMEM((D, PB), BF16),
+            pltpu.VMEM((8 * SB, 8 * TB), BF16),
+            pltpu.VMEM((SB, TB), F32),
+            dma((5,)),
             pltpu.VMEM((NA, D, PB), BF16),
             pltpu.VMEM((TROWS, D), BF16),
             pltpu.VMEM((SROWS, D), BF16),

time: 79.7 us -> 74.8 us (0.939)
  Pallas kernels: 79 us -> 74.1 us
    pallas_call x1, Pallas kernels: 77.1 us -> 72.2 us  [shards(): pl.pallas_call(kernel, out_shape=(jax.ShapeDtypeStruct((2, SB, OUTW), F32...]
where the time goes in v3:
time: 74.8 us; the launch traced here: 74.7 us
  Pallas kernels  74.1 us (99%)
    pallas_call x1, Pallas kernels, shards(): pl.pallas_call(kernel, out_shape=(jax.ShapeDtypeStruct((2, SB, OUTW), F32...  72.2 us
    pallas_call x1, Pallas kernels, shards(): pl.pallas_call(write_out, out_shape=(jax.ShapeDtypeStruct((2 * IMG, CROPS...  1.84 us

profile of v3, /device:TPU:1, one launch (start us, length us, event | category | flops | bytes accessed | tf_op | source)
XLA Modules:
  0.0 74.7 jit_solution(109649734894051261)
XLA Ops:
  0.6 72.2 %head_step.1 = (f32[2,64,384]{2,1,0:T(8,128)}, f32[256,256]{1,0:T(8,128)}) custom-call(bf16[12,2,256]{2,1,0:T(2,128)(2,1)} %t_hbm.1, bf16[10,12,256]{2,1,0:T(8,128)(2,1)} %bitcast.2, bf16[256,256]{1,0:T(8,128)(2,1)} %p_hbm.1, bf16[512,128]{1,0:T(8,128)(2,1)} %constant.4.clone.mix_big_hbm, f32[64,16]{1,0:T(8,128)} %constant.5.clone.mix_hbm), custom_call_target="tpu_custom_call" | custom-call | tf_op jit(solution)/shard_map/head_step/pallas_call | solution.py:499
  72.9 1.8 %write_out.1 = (f32[12,10]{1,0:T(8,128)}, f32[10,12,256]{2,1,0:T(8,128)}, f32[256,256]{1,0:T(8,128)}) custom-call(f32[2,64,384]{2,1,0:T(8,128)} %get-tuple-element.8.out_ref, f32[256,256]{1,0:T(8,128)} %get-tuple-element.9.gv_ref), custom_call_target="tpu_custom_call" | custom-call | tf_op jit(solution)/shard_map/write_out/pallas_call | solution.py:568

commit v4 on v3

--- a/solution.py
+++ b/solution.py
@@ -58,7 +58,7 @@
            t_ref, s_ref, p_ref, mix_big_ref, mix_ref, in_sem,
            wg, tg, sg, k3, kv, e3, st_ref, szt, ub, gb, gs, gx, gz, gr, hb, hx, hz, hr, gw, cs, cr, ys, yr,
            colbuf, rowbuf, zx, zbuf, zown, ztmp, ztot, traw, sraw, at, ats, kvs, uu,
-           w_ss, w_rs, t_ss, t_rs, sz_ss, sz_rs, sx_ss, sx_rs, gx_ss, gx_rs, col_ss, col_rs, row_ss, row_rs, z_ss, z_rs,
+           w_ss, w_rs, tz_ss, tz_rs, tx_ss, tx_rs, sz_ss, sz_rs, sx_ss, sx_rs, gx_ss, gx_rs, col_ss, col_rs, row_ss, row_rs, z_ss, z_rs,
            g_ss, g_rs, h_ss, h_rs, c_ss, c_rs, y_ss, y_rs, o_ss, o_rs,
            k_ss, k_rs, at_ss, at_rs, u_ss, u_rs, zx_ss, zx_rs, hx_ss, hx_rs):
     dp = lax.axis_index("dp")
@@ -97,7 +97,6 @@
         )
 
     comms = {
-        "t": (tg.at[pl.ds(0, (NB - 1) * TB), :], t_ss, t_rs),
         "at": (at, at_ss, at_rs),
         "u": (uu.at[0], u_ss, u_rs),
         "zx": (zx, zx_ss, zx_rs),
@@ -110,8 +109,10 @@
         comms["col%d" % sweep] = (colbuf.at[sweep, pl.ds(0, NA - 1)], col_ss.at[sweep], col_rs.at[sweep])
         comms["row%d" % sweep] = (rowbuf.at[sweep, pl.ds(0, NB - 1)], row_ss.at[sweep], row_rs.at[sweep])
     for z2 in range(1, NZ):
+        comms["tz%d" % z2] = (tg.at[pl.ds(0, TB), :], tz_ss.at[z2 - 1], tz_rs.at[z2 - 1])
         comms["sz%d" % z2] = (sg.at[pl.ds(0, SB), :], sz_ss.at[z2 - 1], sz_rs.at[z2 - 1])
     for o in range(1, NX):
+        comms["tx%d" % o] = (tg.at[pl.ds(0, NZ * TB), :], tx_ss.at[o - 1], tx_rs.at[o - 1])
         comms["sx%d" % o] = (sg.at[pl.ds(0, NZ * SB), :], sx_ss.at[o - 1], sx_rs.at[o - 1])
         comms["gx%d" % o] = (gx.at[o - 1], gx_ss.at[o - 1], gx_rs.at[o - 1])
     for y2 in range(NY):
@@ -174,7 +175,7 @@
     pl.semaphore_wait(barrier, NA - 1 + NB - 1)
 
     w_copies = []
-    for o in (2, 1, 3):
+    for o in (1, 3, 2):
         cp = remote(wg.at[a], wg.at[a], w_ss.at[o - 1], w_rs.at[a], a_dev(a_peer(2 * o)))
         cp.start()
         w_copies.append(cp)
@@ -193,7 +194,17 @@
         remote(src, dst, comms[name][1], comms[name][2], (dp, 1 - c)).start()
 
     t_own = tg.at[rows(b, TB), :]
-    b_all("t", lambda _: t_own, t_own)
+    def t_forward(z2):
+        src = tg.at[rows(x * NZ + z2, TB), :]
+        for o in (2, 1, 3):
+            remote(src, src, tx_ss.at[o - 1], tx_rs.at[o - 1], b_dev(x_peer(o) * NZ + zz)).start()
+
+    for o in (4, 3, 5, 2, 6, 1, 7):
+        started.append("tz%d" % o)
+        remote(t_own, t_own, tz_ss.at[o - 1], tz_rs.at[o - 1], b_dev(x * NZ + z_peer(o))).start()
+    for o in range(1, NX):
+        started.append("tx%d" % o)
+    t_forward(zz)
     cp = remote(wg.at[a], wg.at[a], w_ss.at[NY - 1], w_rs.at[a], (dp, 1 - c))
     cp.start()
     w_copies.append(cp)
@@ -212,7 +223,10 @@
         started.append("sx%d" % o)
     s_forward(zz)
 
-    for o in range(1, NY):
+    for o in (7, 1, 6, 2, 5, 3, 4):
+        recv("tz%d" % o)
+        t_forward(z_peer(NZ - o))
+    for o in (1, 3, 2):
         a2 = a_peer(2 * (NY - o))
         wait_bytes(wg.at[a2], w_rs.at[a2])
         cp = remote(wg.at[a2], wg.at[a2], w_ss.at[NY - 1 + o], w_rs.at[a2], (dp, 1 - c))
@@ -224,7 +238,8 @@
             s_forward(z_peer(NZ - o))
 
     s_on((7, 1, 6, 2))
-    recv("t")
+    for o in range(1, NX):
+        recv("tx%d" % o)
     valid = (lax.broadcasted_iota(jnp.int32, (1, TROWS), 1) % TB < IMG * TEACH).astype(F32)
 
     def set_u(u_row):
@@ -266,21 +281,24 @@
             part = jnp.sum(k3[i] * jnp.concatenate([u2, u2], axis=1), axis=0, keepdims=True)
             colbuf[sweep, a, :, rows(i, PB)] = part
 
-    def row_part(sweep, v, last):
+    def row_part(sweep, v):
         @pl.loop(0, TROWS // 128)
         def _(r):
             acc = jnp.zeros((128, 128), F32)
-            h = jnp.zeros((128, D), F32)
             for i in range(NA):
                 scaled = k3[i, rows(r, 128), :] * v[:, i * PB:(i + 1) * PB]
                 acc = acc + scaled[:, :128] + scaled[:, 128:]
-                if last:
-                    scaled = scaled.astype(BF16)
-                    kv[i, rows(r, 128), :] = scaled
-                    h = h + dot(scaled, wg[i], ((1,), (1,)))
             rowbuf[sweep, b, :, rows(r, 128)] = jnp.sum(acc.T, axis=0, keepdims=True)
-            if last:
-                hb[rows(r, 128), :] = h.astype(BF16)
+
+    def teacher_grad(v):
+        @pl.loop(0, TROWS // 256)
+        def _(r):
+            h = jnp.zeros((256, D), F32)
+            for i in range(NA):
+                scaled = (k3[i, rows(r, 256), :] * v[:, i * PB:(i + 1) * PB]).astype(BF16)
+                kv[i, rows(r, 256), :] = scaled
+                h = h + dot(scaled, wg[i], ((1,), (1,)))
+            hb[rows(r, 256), :] = h.astype(BF16)
 
     def targets(i):
         k = jnp.exp2(dot(tg[...], wg[i]) * (LOG2E / teacher_temp))
@@ -325,7 +343,7 @@
     targets(a)
     for o in range(1, NY):
         targets(a_peer(2 * (NY - o)))
-    for o in (0, 3, 2, 1):
+    for o in (0, 3, 1, 2):
         a2 = ((y + o) % NY) * 2 + 1 - c
         wait_bytes(wg.at[a2], w_rs.at[a2])
         targets(a2)
@@ -333,7 +351,7 @@
     s_on((5, 3, 4))
     student_step(0)
     v = col_wait(0)
-    row_part(0, v, False)
+    row_part(0, v)
     row_send(0)
     student_step(1)
     student_step(3)
@@ -347,29 +365,20 @@
     for o in range(1, NX):
         remote(zown, zx.at[o - 1], zx_ss, zx_rs, b_dev(x_peer(o) * NZ + zz)).start()
     v = col_wait(1)
-    row_part(1, v, False)
+    row_part(1, v)
     row_send(1)
     recv("zx")
     ztmp[...] = zown[...] + zx[0] + zx[1] + zx[2]
+    started.append("z")
+    for o in z_order:
+        remote(ztmp, zbuf.at[o - 1], z_ss, z_rs, b_dev(x * NZ + z_peer(o))).start()
     set_u(row_wait(1))
     col_part(2)
     col_send(2)
     student_send(2)
-    started.append("z")
-    for o in z_order:
-        remote(ztmp, zbuf.at[o - 1], z_ss, z_rs, b_dev(x * NZ + z_peer(o))).start()
     for j in range(TROWS // 128):
         at[:, j * 128:(j + 1) * 128] = dot(st_ref[:, j * 512:(j + 1) * 512], mix_big_ref[...])
     to_sibling("at", at, ats)
-    v = col_wait(2)
-    row_part(2, v, True)
-    row_send(2)
-    started.append("hx")
-    for o in range(1, NX):
-        remote(hb.at[rows(x_peer(o), NZ * TB), :], hx.at[o - 1], hx_ss, hx_rs,
-               b_dev(x_peer(o) * NZ + zz)).start()
-    for y2 in range(NY):
-        to_sibling("k%d" % y2, kv.at[y2 * 2 + 1 - c], kvs.at[y2])
     recv("z")
     zsum = ztmp[...]
     for i in range(NZ - 1):
@@ -385,6 +394,16 @@
         to_sibling("c%d" % y2, cs.at[y2], cr.at[y2])
     for y2 in range(NY):
         gw[y2] = dot(szt[...], e3[y2 * 2 + c])
+    v = col_wait(2)
+    row_part(2, v)
+    row_send(2)
+    teacher_grad(v)
+    started.append("hx")
+    for o in range(1, NX):
+        remote(hb.at[rows(x_peer(o), NZ * TB), :], hx.at[o - 1], hx_ss, hx_rs,
+               b_dev(x_peer(o) * NZ + zz)).start()
+    for y2 in range(NY):
+        to_sibling("k%d" % y2, kv.at[y2 * 2 + 1 - c], kvs.at[y2])
     for o in range(1, NX):
         recv("gx%d" % o)
     started.append("g")
@@ -396,6 +415,23 @@
         gz[o] = g.astype(BF16)
         if o:
             remote(gz.at[o], gr.at[o - 1], g_ss, g_rs, b_dev(x * NZ + z2)).start()
+    u_row = row_wait(2)
+    uu[c] = u_row
+    to_sibling("u", uu.at[c], uu.at[c])
+    set_u(u_row)
+
+    def scaled_mix(mixed_t, u2):
+        full = mixed_t * u2
+        high = full.astype(BF16)
+        return jnp.concatenate([high, (full - high.astype(F32)).astype(BF16)], axis=0)
+
+    def teacher_part(ua, k2):
+        both = dot(ua, k2)
+        return both[:D] + both[D:]
+
+    ua = scaled_mix(at[...], u_row)
+    for y2 in range(NY):
+        gw[y2] = gw[y2] - teacher_part(ua, kv[y2 * 2 + c])
     recv("hx")
     started.append("h")
     for o in z_order + [0]:
@@ -406,23 +442,6 @@
         hz[o] = h.astype(BF16)
         if o:
             remote(hz.at[o], hr.at[o - 1], h_ss, h_rs, b_dev(x * NZ + z2)).start()
-    u_row = row_wait(2)
-    uu[c] = u_row
-    to_sibling("u", uu.at[c], uu.at[c])
-    set_u(u_row)
-
-    def scaled_mix(mixed_t, u2):
-        full = mixed_t * u2
-        high = full.astype(BF16)
-        return jnp.concatenate([high, (full - high.astype(F32)).astype(BF16)], axis=0)
-
-    def teacher_part(ua, k2):
-        both = dot(ua, k2)
-        return both[:D] + both[D:]
-
-    ua = scaled_mix(at[...], u_row)
-    for y2 in range(NY):
-        gw[y2] = gw[y2] - teacher_part(ua, kv[y2 * 2 + c])
     recv("at")
     recv("u")
     ua = scaled_mix(ats[...], uu[1 - c])
@@ -548,7 +567,7 @@
             pltpu.VMEM((NY, TROWS, PB), BF16),
             pltpu.VMEM((2, 1, TROWS), F32),
             dma((2 * NY - 1,)), dma((NA,)),
-            dma, dma,
+            dma((NZ - 1,)), dma((NZ - 1,)), dma((NX - 1,)), dma((NX - 1,)),
             dma((NZ - 1,)), dma((NZ - 1,)), dma((NX - 1,)), dma((NX - 1,)),
             dma((NX - 1,)), dma((NX - 1,)),
             dma((SWEEPS,)), dma((SWEEPS,)), dma((SWEEPS,)), dma((SWEEPS,)),

time: 74.8 us -> 71.5 us (0.956)
  Pallas kernels: 74.1 us -> 70.8 us
    pallas_call x1, Pallas kernels: 72.2 us -> 68.9 us  [shards(): pl.pallas_call(kernel, out_shape=(jax.ShapeDtypeStruct((2, SB, OUTW), F32...]
where the time goes in v4:
time: 71.5 us; the launch traced here: 71.4 us
  Pallas kernels  70.8 us (99%)
    pallas_call x1, Pallas kernels, shards(): pl.pallas_call(kernel, out_shape=(jax.ShapeDtypeStruct((2, SB, OUTW), F32...  68.9 us
    pallas_call x1, Pallas kernels, shards(): pl.pallas_call(write_out, out_shape=(jax.ShapeDtypeStruct((2 * IMG, CROPS...  1.84 us

profile of v4, /device:TPU:1, one launch (start us, length us, event | category | flops | bytes accessed | tf_op | source)
XLA Modules:
  0.0 71.4 jit_solution(13509862641919361623)
XLA Ops:
  0.6 68.9 %head_step.1 = (f32[2,64,384]{2,1,0:T(8,128)}, f32[256,256]{1,0:T(8,128)}) custom-call(bf16[12,2,256]{2,1,0:T(2,128)(2,1)} %t_hbm.1, bf16[10,12,256]{2,1,0:T(8,128)(2,1)} %bitcast.2, bf16[256,256]{1,0:T(8,128)(2,1)} %p_hbm.1, bf16[512,128]{1,0:T(8,128)(2,1)} %constant.4.clone.mix_big_hbm, f32[64,16]{1,0:T(8,128)} %constant.5.clone.mix_hbm), custom_call_target="tpu_custom_call" | custom-call | tf_op jit(solution)/shard_map/head_step/pallas_call | solution.py:518
  69.5 1.8 %write_out.1 = (f32[12,10]{1,0:T(8,128)}, f32[10,12,256]{2,1,0:T(8,128)}, f32[256,256]{1,0:T(8,128)}) custom-call(f32[2,64,384]{2,1,0:T(8,128)} %get-tuple-element.8.out_ref, f32[256,256]{1,0:T(8,128)} %get-tuple-element.9.gv_ref), custom_call_target="tpu_custom_call" | custom-call | tf_op jit(solution)/shard_map/write_out/pallas_call | solution.py:587

commit v5 on v4

--- a/solution.py
+++ b/solution.py
@@ -432,16 +432,6 @@
     ua = scaled_mix(at[...], u_row)
     for y2 in range(NY):
         gw[y2] = gw[y2] - teacher_part(ua, kv[y2 * 2 + c])
-    recv("hx")
-    started.append("h")
-    for o in z_order + [0]:
-        z2 = z_peer(o)
-        h = hb[rows(x * NZ + z2, TB), :].astype(F32)
-        for i in range(NX - 1):
-            h = h + hx[i, rows(z2, TB), :].astype(F32)
-        hz[o] = h.astype(BF16)
-        if o:
-            remote(hz.at[o], hr.at[o - 1], h_ss, h_rs, b_dev(x * NZ + z2)).start()
     recv("at")
     recv("u")
     ua = scaled_mix(ats[...], uu[1 - c])
@@ -459,22 +449,34 @@
         else:
             gw[y2] = both
 
+    recv("hx")
+    started.append("h")
+    for o in z_order + [0]:
+        z2 = z_peer(o)
+        h = hb[rows(x * NZ + z2, TB), :].astype(F32)
+        for i in range(NX - 1):
+            h = h + hx[i, rows(z2, TB), :].astype(F32)
+        hz[o] = h.astype(BF16)
+        if o:
+            remote(hz.at[o], hr.at[o - 1], h_ss, h_rs, b_dev(x * NZ + z2)).start()
+
+    recv("g")
+    g = gz[0].astype(F32)
+    for i in range(NZ - 1):
+        g = g + gr[i].astype(F32)
+    u_own = ub[rows(b, TB), :]
+    u_own = jnp.concatenate([u_own, u_own], axis=1)
+    ub[0:128, :] = column(ztot[:, rows(b // 2, 128)])
+    z_own = ub[rows(b % 2, SB), :]
+    g = g / jnp.concatenate([z_own, z_own], axis=1)
     recv("h")
     h = hz[0].astype(F32)
     for i in range(NZ - 1):
         h = h + hr[i].astype(F32)
-    u_own = ub[rows(b, TB), :]
-    mixed = dot(mix_ref[...], h * jnp.concatenate([u_own, u_own], axis=1),
-                precision=lax.Precision.HIGHEST)
-    recv("g")
-    g = gz[0].astype(F32)
-    for i in range(NZ - 1):
-        g = g + gr[i].astype(F32)
-    ub[0:128, :] = column(ztot[:, rows(b // 2, 128)])
-    z_own = ub[rows(b % 2, SB), :]
+    mixed = dot(mix_ref[...], h * u_own, precision=lax.Precision.HIGHEST)
     student_f = s_raw / snorm
     student_b = student_f.astype(BF16).astype(F32)
-    grad_n = (g / jnp.concatenate([z_own, z_own], axis=1) - mixed) / student_temp
+    grad_n = (g - mixed) / student_temp
     loss = jnp.log(z_own) - jnp.sum(student_b * mixed, axis=1, keepdims=True) / student_temp
     grad_s = (grad_n - student_f * jnp.sum(student_f * grad_n, axis=1, keepdims=True)) / snorm
     out_ref[c, :, 0:D] = grad_s

time: 71.5 us -> 72 us (level)
  no operation moved by 1% of the time
where the time goes in v5:
time: 72 us; the launch traced here: 71.9 us
  Pallas kernels  71.3 us (99%)
    pallas_call x1, Pallas kernels, shards(): pl.pallas_call(kernel, out_shape=(jax.ShapeDtypeStruct((2, SB, OUTW), F32...  69.4 us
    pallas_call x1, Pallas kernels, shards(): pl.pallas_call(write_out, out_shape=(jax.ShapeDtypeStruct((2 * IMG, CROPS...  1.84 us

profile of v5, /device:TPU:1, one launch (start us, length us, event | category | flops | bytes accessed | tf_op | source)
XLA Modules:
  0.0 71.9 jit_solution(6484496930075544520)
XLA Ops:
  0.6 69.4 %head_step.1 = (f32[2,64,384]{2,1,0:T(8,128)}, f32[256,256]{1,0:T(8,128)}) custom-call(bf16[12,2,256]{2,1,0:T(2,128)(2,1)} %t_hbm.1, bf16[10,12,256]{2,1,0:T(8,128)(2,1)} %bitcast.2, bf16[256,256]{1,0:T(8,128)(2,1)} %p_hbm.1, bf16[512,128]{1,0:T(8,128)(2,1)} %constant.4.clone.mix_big_hbm, f32[64,16]{1,0:T(8,128)} %constant.5.clone.mix_hbm), custom_call_target="tpu_custom_call" | custom-call | tf_op jit(solution)/shard_map/head_step/pallas_call | solution.py:520
  70.1 1.8 %write_out.1 = (f32[12,10]{1,0:T(8,128)}, f32[10,12,256]{2,1,0:T(8,128)}, f32[256,256]{1,0:T(8,128)}) custom-call(f32[2,64,384]{2,1,0:T(8,128)} %get-tuple-element.8.out_ref, f32[256,256]{1,0:T(8,128)} %get-tuple-element.9.gv_ref), custom_call_target="tpu_custom_call" | custom-call | tf_op jit(solution)/shard_map/write_out/pallas_call | solution.py:589
